TPU v7x, 32 devices: a whole 2x2x4 slice. The times are simulated.
32 devices in a mesh: dp: 8 (over y, x, core), head: 4 (over z).
Axes of the slice: x: 2, y: 2, z: 4, core: 2. Of those that a mesh axis runs over, the one named last changes fastest.
Arguments:
- tokens: bfloat16 [16384, 1024], P(('dp', 'head')), may hold values from -6 to 6
- attn_query: bfloat16 [1024, 1024], P(None, 'head'), may hold values from -0.1875 to 0.1875
- attn_key: bfloat16 [1024, 1024], P(None, 'head'), may hold values from -0.1875 to 0.1875
- attn_value: bfloat16 [1024, 1024], P(None, 'head'), may hold values from -0.1875 to 0.1875
- attn_gate: bfloat16 [1024, 1024], P(None, 'head'), may hold values from -0.1875 to 0.1875
- attn_out: bfloat16 [1024, 1024], P('head'), may hold values from -0.1875 to 0.1875
- rotation_rates: float32 [1024], P('head'), may hold values from 0.0005 to 1
- ffn_left: bfloat16 [1024, 2816], P(None, 'head'), may hold values from -0.1875 to 0.1875
- ffn_right: bfloat16 [1024, 2816], P(None, 'head'), may hold values from -0.1875 to 0.1875
- ffn_down: bfloat16 [2816, 1024], P('head'), may hold values from -0.109375 to 0.109375
- out_grad: bfloat16 [16384, 1024], P(('dp', 'head')), may hold values from -6 to 6
Outputs:
- block_out: bfloat16 [16384, 1024], P(('dp', 'head'))
- input_grad: float32 [16384, 1024], P(('dp', 'head'))
- query_grad: float32 [1024, 1024], P(None, 'head')
- key_grad: float32 [1024, 1024], P(None, 'head')
- value_grad: float32 [1024, 1024], P(None, 'head')
- gate_grad: float32 [1024, 1024], P(None, 'head')
- out_proj_grad: float32 [1024, 1024], P('head')
- rates_grad: float32 [1024], P('head')
- left_grad: float32 [1024, 2816], P(None, 'head')
- right_grad: float32 [1024, 2816], P(None, 'head')
- down_grad: float32 [2816, 1024], P('head')
All inputs are finite; a program needn't handle non-finite values.
Results may differ from a plain program's by a relative error of at most 0.025.
The roundings to bfloat16 on the way count: a program that leaves them out, or rounds other values in their place, can miss the bound.
Values may be sent and summed in bfloat16 or wider, within the bound.
A program may use at most 192 MiB of HBM per device.

v0:
```python
import functools

import jax
import jax.numpy as jnp
from jax import lax
from jax.experimental import pallas as pl
from jax.experimental.pallas import tpu as pltpu
from jax.sharding import PartitionSpec as P

HEADS = 8
HEAD_DIM = 128
SPAN = 256
EPSILON = 1e-06
BF = jnp.bfloat16
F32 = jnp.float32


MESH = pl.DeviceIdType.MESH
ANY = pl.BlockSpec(memory_space=pl.ANY)
IN_VMEM = pl.BlockSpec(memory_space=pltpu.VMEM)


def split(value):
    high = value.astype(BF)
    return high, (value - high.astype(F32)).astype(BF)


class Place:
    def __init__(self, n_head):
        self.n_head = n_head
        dp = lax.axis_index("dp")
        self.z = lax.axis_index("head")
        self.core = lax.rem(dp, 2)
        x = lax.rem(lax.div(dp, 2), 2)
        y = lax.rem(lax.div(dp, 4), 2)
        self.plane = x + 2 * y
        self.at = [self.plane, self.plane + 1 - 2 * x, self.plane + 2 - 4 * y, 3 - self.plane]
        self.across = {"dp": dp + 1 - 2 * self.core}
        self.by_x = {"dp": dp + 2 - 4 * x}
        self.by_y = {"dp": dp + 4 - 8 * y}
        self.up = {"head": lax.rem(self.z + 1, n_head)}
        self.down = {"head": lax.rem(self.z + n_head - 1, n_head)}

    def above(self, step):
        return {"head": lax.rem(self.z + step, self.n_head)}

    def below(self, step):
        return {"head": lax.rem(self.z + self.n_head - step, self.n_head)}

    def greet(self):
        others = [self.across, self.by_x, self.by_y]
        others += [self.below(step) for step in range(1, self.n_head)]
        for other in others:
            barrier = pltpu.get_barrier_semaphore()
            pl.semaphore_signal(barrier, inc=1, device_id=other, device_id_type=MESH)

    def meet(self):
        pl.semaphore_wait(pltpu.get_barrier_semaphore(), self.n_head + 2)


class Copies:
    def __init__(self, sends, receives, locals_):
        self.sends, self.receives, self.locals = sends, receives, locals_
        self.pending = []
        self.started = {}
        self.n_local = 0

    def send(self, src, dst, out, into, device, when=None):
        copy = pltpu.make_async_remote_copy(
            src_ref=src,
            dst_ref=dst,
            send_sem=self.sends.at[out],
            recv_sem=self.receives.at[into],
            device_id=device,
            device_id_type=MESH,
        )
        if when is None:
            copy.start()
            self.pending.append(copy.wait_send)
            if isinstance(out, int):
                self.started[out] = copy.wait_send
        else:
            pl.when(when)(copy.start)
            self.pending.append(lambda: pl.when(when)(copy.wait_send))

    def receive(self, dst, into, device):
        pltpu.make_async_remote_copy(
            src_ref=dst,
            dst_ref=dst,
            send_sem=self.sends.at[0],
            recv_sem=self.receives.at[into],
            device_id=device,
            device_id_type=MESH,
        ).wait_recv()

    def move(self, src, dst, later=False):
        copy = pltpu.make_async_copy(src, dst, self.locals.at[self.n_local])
        self.n_local += 1
        copy.start()
        if later:
            self.pending.append(copy.wait)
        return copy

    def sent(self, out):
        wait = self.started.pop(out)
        self.pending.remove(wait)
        wait()

    def finish(self):
        for wait in self.pending:
            wait()


class Gather:
    def __init__(self, place, copies, view, base, late=None):
        self.place, self.copies, self.view, self.base = place, copies, view, base
        self.late = late

    def begin(self):
        place, z = self.place, self.place.z
        own = self.view(0, 0, None)
        last = place.n_head - 1
        self.copies.send(
            own, self.view(last, 0, None), self.base, self.base + last, place.up, when=z < last
        )
        self.copies.send(own, self.view(1, 0, None), self.base + 1, self.base + 1, place.down, when=z > 0)

    def arrived(self, slot, when=True):
        place, copies, z, base = self.place, self.copies, self.place.z, self.base
        last = place.n_head - 1
        if when is True:
            copies.receive(self.view(slot, 0, None), base + slot, place.up)
        else:
            pl.when(when)(lambda: copies.receive(self.view(slot, 0, None), base + slot, place.up))
        from_up = z + slot <= last
        piece = self.view(slot, 0, None)
        down = jnp.logical_and(jnp.logical_and(from_up, z > 0), when)
        up = jnp.logical_and(jnp.logical_not(from_up), z < last)
        up = jnp.logical_and(up, when)
        always = None if when is True else when
        after = jnp.minimum(slot + 1, last)
        before = jnp.maximum(slot - 1, 1)
        copies.send(piece, self.view(after, 0, None), base + 1 + slot, base + after, place.down, when=down)
        copies.send(piece, self.view(before, 0, None), base + 1 + slot, base + before, place.up, when=up)
        at = base + 4 * slot + 4
        copies.send(piece, self.view(slot, 1, None), at, at, place.by_x, when=always)
        copies.send(piece, self.view(slot, 2, None), at + 1, at + 1, place.by_y, when=always)

    def spread(self, slot):
        place, copies = self.place, self.copies
        at = self.base + 4 * slot + 4
        now = None if self.late is None else slot != self.late
        low, high = self.view(slot, 3, 0), self.view(slot, 3, 1)
        copies.receive(self.view(slot, 1, None), at, place.by_x)
        copies.send(self.view(slot, 1, 0), low, at + 2, at + 2, place.by_y, when=now)
        copies.receive(self.view(slot, 2, None), at + 1, place.by_y)
        copies.send(self.view(slot, 2, 1), high, at + 3, at + 3, place.by_x, when=now)

    def complete(self, slot):
        place, copies = self.place, self.copies
        at = self.base + 4 * slot + 4

        def receive():
            copies.receive(self.view(slot, 3, 0), at + 2, place.by_y)
            copies.receive(self.view(slot, 3, 1), at + 3, place.by_x)

        if self.late is None:
            receive()
        else:
            pl.when(slot != self.late)(receive)


PER_GATHER = 24


def forward_kernel(
    n_head,
    tokens,
    out_grad,
    wq,
    wk,
    wv,
    wg,
    wo,
    ffn_left,
    ffn_right,
    ffn_down,
    rates,
    wa_out,
    wo_out,
    wf_out,
    nin_out,
    pre_out,
    q_out,
    k_out,
    v_out,
    attn_out,
    cos_out,
    sin_out,
    fresh_out,
    carry_out,
    scale_out,
    gated_out,
    hidden_out,
    nm_out,
    og_out,
    wa_ref,
    wo_ref,
    wf_ref,
    x_ref,
    nin_ref,
    pre_ref,
    q_ref,
    k_ref,
    v_ref,
    attn_ref,
    cos_ref,
    sin_ref,
    fresh_ref,
    carry_ref,
    message_ref,
    squares_ref,
    other_squares_ref,
    gated_ref,
    branch_ref,
    other_branch_ref,
    hidden_ref,
    nm_ref,
    rates_ref,
    og_ref,
    sends,
    receives,
    locals_,
):
    rows, width = tokens.shape
    quarter = width // 4
    units = ffn_down.shape[0] // 2
    tiles = 2 * rows // SPAN
    place = Place(n_head)
    z, core = place.z, place.core
    last = n_head - 1
    place.greet()
    copies = Copies(sends, receives, locals_)

    def columns(start, size):
        return pl.ds(pl.multiple_of(start, size), size)

    def own_weights(q):
        far = columns(place.at[q] * quarter, quarter)
        near = pl.ds(q * quarter, quarter)
        loads = []
        for i, w in enumerate((wq, wk, wv, wg)):
            src = w.at[far, columns(core * HEAD_DIM, HEAD_DIM)]
            loads.append(copies.move(src, wa_ref.at[0, near, pl.ds(i * HEAD_DIM, HEAD_DIM)]))
        src = wo.at[columns(core * HEAD_DIM, HEAD_DIM), far]
        loads.append(copies.move(src, wo_ref.at[pl.ds(0, HEAD_DIM), near]))
        for i, w in enumerate((ffn_left, ffn_right, ffn_down)):
            src = w.at[pl.ds(pl.multiple_of(core * units, 16), units), far]
            loads.append(copies.move(src, wf_ref.at[i, pl.ds(0, units), near]))
        return loads

    own_loads = [own_weights(0)]
    token_loads = [
        copies.move(
            tokens.at[:, columns(place.at[q] * quarter, quarter)],
            x_ref.at[:, pl.ds(q * quarter, quarter)],
        )
        for q in range(4)
    ]
    place.meet()

    def half_rows(half, size):
        return pl.ds(0, size) if half is None else pl.ds(half * (size // 2), size // 2)

    def wa_view(part, slot, q, half):
        at = half_rows(half, quarter)
        lanes = pl.ds(part * 2 * HEAD_DIM, 2 * HEAD_DIM)
        return wa_ref.at[slot, pl.ds(q * quarter + at.start, at.size), lanes]

    def wo_view(slot, q, half):
        at = half_rows(half, HEAD_DIM)
        return wo_ref.at[
            pl.ds(pl.multiple_of(slot * HEAD_DIM + at.start, HEAD_DIM // 2), at.size),
            pl.ds(q * quarter, quarter),
        ]

    def wf_view(slot, q, half):
        at = half_rows(half, units)
        return wf_ref.at[
            :,
            pl.ds(pl.multiple_of(slot * units + at.start, 16), at.size),
            pl.ds(q * quarter, quarter),
        ]

    attn_all = [
        Gather(place, copies, functools.partial(wa_view, part), part * PER_GATHER)
        for part in range(2)
    ]
    attn_all.append(Gather(place, copies, wo_view, 2 * PER_GATHER))
    feed = Gather(place, copies, wf_view, 3 * PER_GATHER, late=last)
    base = 4 * PER_GATHER
    for loads, part in zip((own_loads[0][:2], own_loads[0][2:4], own_loads[0][4:5]), attn_all):
        for load in loads:
            load.wait()
        part.begin()
    grad_loads = [
        copies.move(
            out_grad.at[:, columns(place.at[q] * quarter, quarter)],
            og_ref.at[pl.ds(0, rows), pl.ds(q * quarter, quarter)],
        )
        for q in range(4)
    ]
    own_loads += [own_weights(q) for q in range(1, 4)]
    for step in range(1, n_head):
        copies.send(rates, rates_ref.at[step], base + step, base + step, place.below(step))
    rates_ref[0] = rates[...]

    for load in token_loads:
        load.wait()

    def norm_rows(values):
        mean = jnp.mean(values * values, axis=-1, keepdims=True)
        return values * lax.rsqrt(mean + EPSILON)

    @pl.loop(0, rows // 128)
    def _(i):
        at = pl.ds(pl.multiple_of(i * 128, 128), 128)
        nin_ref[at, :] = norm_rows(x_ref[at, :].astype(F32)).astype(BF)

    base += 4
    for load in grad_loads:
        load.wait()
    og_other = og_ref.at[pl.ds(rows, rows)]
    copies.send(og_ref.at[pl.ds(0, rows)], og_other, base, base, place.across)
    base += 1
    nin_other = nin_ref.at[pl.ds(rows, rows)]
    copies.send(nin_ref.at[pl.ds(0, rows)], nin_other, base, base, place.across)
    for q, loads in enumerate(own_loads):
        for load in loads[5:] if q == 0 else loads:
            load.wait()
    for step in range(1, n_head):
        copies.receive(rates_ref.at[step], base - 5 + step, place.up)
    copies.receive(nin_other, base, place.across)
    copies.move(nin_ref, nin_out, later=True)
    own_rows = pl.ds(0, units)
    copies.move(wf_ref.at[:, own_rows], wf_out.at[:, own_rows], later=True)
    copies.receive(og_other, base - 1, place.across)
    copies.move(og_ref, og_out, later=True)

    def decay_of(head):
        exponent = jnp.full((1, 1), -8.0 / HEADS, F32) * (head + 1).astype(F32)
        return jnp.exp2(exponent)

    def tile(i):
        return pl.ds(pl.multiple_of(i * SPAN, SPAN), SPAN)

    def iota(shape, axis):
        return lax.broadcasted_iota(jnp.int32, shape, axis).astype(F32)

    def dot(left, right):
        return jnp.dot(left, right, preferred_element_type=F32)

    def slot_compute(slot):
        head = 2 * lax.rem(z + slot, n_head) + core
        decay = decay_of(head)
        rate = rates_ref[slot, :, columns(core * HEAD_DIM, HEAD_DIM)]
        coarse = (z * rows).astype(F32) + 32.0 * iota((rows // 32, HEAD_DIM), 0)
        coarse = coarse * rate
        fine = iota((32, HEAD_DIM), 0) * rate
        cos_a, sin_a = jnp.cos(coarse), jnp.sin(coarse)
        cos_b, sin_b = jnp.cos(fine), jnp.sin(fine)
        for a in range(rows // 32):
            cos_row, sin_row = cos_a[a : a + 1], sin_a[a : a + 1]
            cos_ref[slot, pl.ds(a * 32, 32), :] = cos_row * cos_b - sin_row * sin_b
            sin_ref[slot, pl.ds(a * 32, 32), :] = sin_row * cos_b + cos_row * sin_b
        offsets = iota((SPAN, SPAN), 0) - iota((SPAN, SPAN), 1)
        mask = jnp.where(offsets >= 0.0, jnp.exp(-decay * jnp.maximum(offsets, 0.0)), 0.0)
        late = jnp.exp(-decay * (SPAN - 1.0 - iota((SPAN, HEAD_DIM), 0)))

        @pl.loop(0, tiles)
        def _(i):
            at = tile(i)
            pre = dot(nin_ref[at, :], wa_ref[slot])
            pre_ref[slot, at, :] = pre
            here = tile(lax.rem(i, rows // SPAN))
            cosines, sines = cos_ref[slot, here, :], sin_ref[slot, here, :]

            def rotate(values):
                activated = values / (1.0 + jnp.exp(-values))
                turned = jnp.concatenate([activated * cosines, activated * sines], axis=1)
                return turned.astype(BF)

            query = rotate(pre[:, :HEAD_DIM])
            keys = rotate(pre[:, HEAD_DIM : 2 * HEAD_DIM])
            value = pre[:, 2 * HEAD_DIM : 3 * HEAD_DIM].astype(BF)
            q_ref[slot, at, :] = query
            k_ref[slot, at, :] = keys
            v_ref[slot, at, :] = value
            scores = lax.dot_general(
                query, keys, (((1,), (1,)), ((), ())), preferred_element_type=F32
            )
            weights = (scores * mask).astype(BF)
            attn_ref[slot, at, :] = dot(weights, value)
            high, low = split(value.astype(F32) * late)
            both = lax.dot_general(
                keys,
                jnp.concatenate([high, low], axis=1),
                (((0,), (0,)), ((), ())),
                preferred_element_type=F32,
            )
            fresh_ref[slot, i] = both[:, :HEAD_DIM] + both[:, HEAD_DIM:]

        for ref, out in (
            (wa_ref, wa_out),
            (pre_ref, pre_out),
            (q_ref, q_out),
            (k_ref, k_out),
            (v_ref, v_out),
            (cos_ref, cos_out),
            (sin_ref, sin_out),
            (fresh_ref, fresh_out),
        ):
            copies.move(ref.at[slot], out.at[slot], later=True)

    first = 1 + 2 * lax.div(z, last)
    second = 2 + lax.rem(lax.div(z + 1, 2), 2)
    third = 6 - first - second

    for part in attn_all:
        part.arrived(first)
    slot_compute(0)
    for part in attn_all:
        part.arrived(second)
    for part in attn_all:
        part.spread(first)
    for part in attn_all:
        part.arrived(third)
    feed.begin()
    for part in attn_all:
        part.spread(second)
    for part in attn_all[:2]:
        part.complete(first)
    slot_compute(first)
    for part in attn_all:
        part.spread(third)
    feed.arrived(first)
    for part in attn_all[:2]:
        part.complete(second)
    slot_compute(second)
    inner = jnp.logical_and(z > 0, z < last)
    feed.arrived(second, inner)
    for part in attn_all[:2]:
        part.complete(third)
    slot_compute(third)
    base += 1
    chain_base = base
    n_chain = 2 * n_head

    def chain_at(index):
        group, seq = lax.div(index, 2), lax.rem(index, 2)
        return lax.rem(group - z + n_head, n_head), seq, decay_of(2 * group + core)

    def chain_copy(index, slot, seq):
        after = lax.rem(slot + n_head - 1, n_head)
        return pltpu.make_async_remote_copy(
            src_ref=message_ref.at[slot, seq],
            dst_ref=carry_ref.at[after, seq],
            send_sem=sends.at[chain_base + index],
            recv_sem=receives.at[chain_base + index],
            device_id=place.up,
            device_id_type=MESH,
        )

    def hand_on(index, slot, seq, decay):
        total = jnp.exp(-decay * rows) * carry_ref[slot, seq].astype(F32)
        for n in range(rows // SPAN):
            left = rows - (n + 1) * SPAN
            total += jnp.exp(-decay * left) * fresh_ref[slot, seq * (rows // SPAN) + n]
        message_ref[slot, seq] = total.astype(BF)
        chain_copy(index, slot, seq).start()

    @pl.when(z == 0)
    def _():
        @pl.loop(0, n_chain)
        def _(index):
            slot, seq, decay = chain_at(index)
            carry_ref[slot, seq] = jnp.zeros(carry_ref.shape[2:], BF)
            hand_on(index, slot, seq, decay)

    feed.arrived(second, jnp.logical_not(inner))
    feed.spread(first)
    feed.arrived(third)

    @pl.when(z > 0)
    def _():
        @pl.loop(0, n_chain)
        def _(index):
            slot, seq, decay = chain_at(index)
            copies.receive(carry_ref.at[slot, seq], chain_base + index, place.down)
            pl.when(z < last)(lambda: hand_on(index, slot, seq, decay))

    copies.move(carry_ref, carry_out, later=True)
    feed.spread(second)

    def feed_done(slot):
        feed.complete(slot)
        at = pl.ds(pl.multiple_of(slot * units, 16), units)
        copies.move(wf_ref.at[:, at], wf_out.at[:, at], later=True)

    def apply(seq):
        mine = pl.ds(seq * rows, rows)
        squares_ref[mine, :] = jnp.zeros((rows, HEAD_DIM), F32)

        @pl.loop(0, n_head)
        def _(slot):
            decay = decay_of(2 * lax.rem(z + slot, n_head) + core)
            early = jnp.exp(-decay * (iota((SPAN, HEAD_DIM), 0) + 1.0))
            state = carry_ref[slot, seq].astype(F32)
            for n in range(rows // SPAN):
                i = seq * (rows // SPAN) + n
                at = pl.ds(i * SPAN, SPAN)
                both = dot(q_ref[slot, at, :], jnp.concatenate(split(state), axis=1))
                attn = attn_ref[slot, at, :]
                attn += early * (both[:, :HEAD_DIM] + both[:, HEAD_DIM:])
                attn_ref[slot, at, :] = attn
                squares_ref[at, :] += jnp.sum(attn * attn, axis=-1, keepdims=True)
                if n + 1 < rows // SPAN:
                    state = jnp.exp(-decay * SPAN) * state + fresh_ref[slot, i]

    def gating(seq):
        for n in range(rows // SPAN):
            at = pl.ds(seq * rows + n * SPAN, SPAN)
            total = squares_ref[at, :] + other_squares_ref[at, :]
            scale = lax.rsqrt(total / width + EPSILON)
            other_squares_ref[at, :] = scale
            for slot in range(n_head):
                gate = pre_ref[slot, at, pl.ds(3 * HEAD_DIM, HEAD_DIM)]
                gated = (attn_ref[slot, at, :] * scale * gate).astype(BF)
                gated_ref[at, pl.ds(slot * HEAD_DIM, HEAD_DIM)] = gated

    base += n_chain
    own, other = pl.ds(0, rows), pl.ds(rows, rows)
    apply(1)
    copies.send(squares_ref.at[other], other_squares_ref.at[own], base, base, place.across)
    apply(0)
    copies.send(squares_ref.at[own], other_squares_ref.at[other], base + 1, base + 1, place.across)
    copies.move(attn_ref, attn_out, later=True)
    for slot in (first, second, third):
        attn_all[2].complete(slot)
    copies.receive(other_squares_ref.at[other], base + 1, place.across)
    gating(1)
    feed_done(first)
    base += 2
    for n in range(rows // SPAN):
        gated = gated_ref[pl.ds(rows + n * SPAN, SPAN), :]
        branch_ref[pl.ds(n * SPAN, SPAN), :] = dot(gated, wo_ref[...]).astype(BF)
    copies.send(branch_ref, other_branch_ref, base, base, place.across)
    copies.receive(other_squares_ref.at[own], base - 2, place.across)
    gating(0)
    copies.move(other_squares_ref, scale_out, later=True)
    copies.move(gated_ref, gated_out, later=True)
    copies.move(wo_ref, wo_out, later=True)
    feed.spread(third)
    feed_done(second)

    @pl.loop(0, rows // SPAN)
    def _(i):
        at = tile(i)
        hidden_ref[at, :] = x_ref[at, :].astype(F32) + dot(gated_ref[at, :], wo_ref[...])

    copies.receive(other_branch_ref, base, place.across)

    @pl.loop(0, rows // 128)
    def _(i):
        at = pl.ds(pl.multiple_of(i * 128, 128), 128)
        hidden = hidden_ref[at, :] + other_branch_ref[at, :].astype(F32)
        hidden_ref[at, :] = hidden
        nm_ref[at, :] = norm_rows(hidden).astype(BF)

    copies.send(nm_ref.at[own], nm_ref.at[other], base + 1, base + 1, place.across)
    copies.move(hidden_ref, hidden_out, later=True)
    feed_done(third)
    copies.receive(nm_ref.at[other], base + 1, place.across)
    copies.move(nm_ref, nm_out, later=True)

    @pl.when(z < last)
    def _():
        @pl.loop(0, n_chain)
        def _(index):
            slot, seq, _ = chain_at(index)
            chain_copy(index, slot, seq).wait_send()

    copies.finish()


def forward(n_head, tokens, out_grad, wq, wk, wv, wg, wo, ffn_left, ffn_right, ffn_down, rates):
    rows, width = tokens.shape
    units = ffn_down.shape[0] // 2
    tall = 2 * rows
    buffers = [
        ((n_head, width, 4 * HEAD_DIM), BF),
        ((n_head * HEAD_DIM, width), BF),
        ((3, n_head * units, width), BF),
        ((rows, width), BF),
        ((tall, width), BF),
        ((n_head, tall, 4 * HEAD_DIM), F32),
        ((n_head, tall, 2 * HEAD_DIM), BF),
        ((n_head, tall, 2 * HEAD_DIM), BF),
        ((n_head, tall, HEAD_DIM), BF),
        ((n_head, tall, HEAD_DIM), F32),
        ((n_head, rows, HEAD_DIM), F32),
        ((n_head, rows, HEAD_DIM), F32),
        ((n_head, tall // SPAN, 2 * HEAD_DIM, HEAD_DIM), F32),
        ((n_head, 2, 2 * HEAD_DIM, HEAD_DIM), BF),
        ((n_head, 2, 2 * HEAD_DIM, HEAD_DIM), BF),
        ((tall, HEAD_DIM), F32),
        ((tall, HEAD_DIM), F32),
        ((tall, n_head * HEAD_DIM), BF),
        ((rows, width), BF),
        ((rows, width), BF),
        ((rows, width), F32),
        ((tall, width), BF),
        ((n_head, 1, 2 * HEAD_DIM), F32),
        ((tall, width), BF),
    ]
    out_of = [0, 1, 2, 4, 5, 6, 7, 8, 9, 10, 11, 12, 13, 16, 17, 20, 21, 23]
    n_sems = 4 * PER_GATHER + 4 + 1 + 1 + 2 * n_head + 2 + 2
    return pl.pallas_call(
        functools.partial(forward_kernel, n_head),
        out_shape=[jax.ShapeDtypeStruct(*buffers[i]) for i in out_of],
        in_specs=[ANY] * 10 + [IN_VMEM],
        out_specs=[ANY] * len(out_of),
        scratch_shapes=[pltpu.VMEM(*b) for b in buffers]
        + [
            pltpu.SemaphoreType.DMA((n_sems,)),
            pltpu.SemaphoreType.DMA((n_sems,)),
            pltpu.SemaphoreType.DMA((96,)),
        ],
        compiler_params=pltpu.CompilerParams(
            collective_id=0, has_side_effects=True, vmem_limit_bytes=62 << 20
        ),
        name="forward",
    )(tokens, out_grad, wq, wk, wv, wg, wo, ffn_left, ffn_right, ffn_down, rates)


class Scatter:
    def __init__(self, place, copies, view, far_x, far_y, near_x, near_y, high, base, items=None):
        self.place, self.copies, self.view, self.base = place, copies, view, base
        self.items = items
        self.far_x, self.far_y, self.near_x, self.near_y, self.high = far_x, far_y, near_x, near_y, high

    def part(self, buffer, slot):
        return buffer.at[slot] if self.items is None else buffer.at[slot, pl.ds(0, self.items(slot))]

    def begin(self, slot):
        place, at = self.place, self.base + 4 * slot
        self.copies.send(self.view(slot, 3, 0), self.part(self.far_y, slot), at, at, place.by_y)
        self.copies.send(self.view(slot, 3, 1), self.part(self.far_x, slot), at + 1, at + 1, place.by_x)

    def middle(self, slot):
        place, copies, at = self.place, self.copies, self.base + 4 * slot
        copies.receive(self.part(self.far_y, slot), at, place.by_y)
        add_to(self.view(slot, 1, 0), self.part(self.far_y, slot))
        copies.send(self.view(slot, 1, None), self.part(self.near_x, slot), at + 2, at + 2, place.by_x)
        copies.receive(self.part(self.far_x, slot), at + 1, place.by_x)
        add_to(self.view(slot, 2, 1), self.part(self.far_x, slot))
        copies.send(self.view(slot, 2, None), self.part(self.near_y, slot), at + 3, at + 3, place.by_y)

    def end(self, slot, onward=True):
        place, copies, at = self.place, self.copies, self.base + 4 * slot
        copies.receive(self.part(self.near_x, slot), at + 2, place.by_x)
        copies.receive(self.part(self.near_y, slot), at + 3, place.by_y)
        add_to(self.view(slot, 0, None), self.part(self.near_x, slot), self.part(self.near_y, slot))
        if slot and onward:
            self.go_up(slot)

    def go_up(self, slot):
        at = self.base + 4 * self.place.n_head + slot
        into = self.high.at[slot - 1]
        self.copies.send(self.view(slot, 0, None), into, at, at, self.place.above(slot))

    def total(self, into=None, slots=(1, 2, 3)):
        place = self.place
        high = [self.high.at[slot - 1] for slot in slots]
        for slot, part in zip(slots, high):
            self.copies.receive(part, self.base + 4 * place.n_head + slot, place.up)
        add_to(self.view(0, 0, None), *high, into=into)


PER_SCATTER = 20


def add_to(ref, *others, into=None):
    def add(into, *refs):
        total = refs[0][...].astype(F32)
        for other in refs[1:]:
            total += other[...].astype(F32)
        into[...] = total.astype(BF)

    refs = (ref if into is None else into, ref) + others
    if len(ref.shape) == 2:
        add(*refs)
    else:
        for i in range(ref.shape[0]):
            add(*(one.at[i] for one in refs))


def dot(left, right):
    return jnp.dot(left, right, preferred_element_type=F32)


def iota(shape, axis):
    return lax.broadcasted_iota(jnp.int32, shape, axis).astype(F32)


def decay_of(head):
    exponent = jnp.full((1, 1), -8.0 / HEADS, F32) * (head + 1).astype(F32)
    return jnp.exp2(exponent)


def middle_kernel(
    n_head,
    wf,
    nm,
    og,
    hidden,
    wo,
    pre,
    query,
    attn,
    scale,
    feed_out,
    block_out,
    hidden_grad_out,
    branch_out,
    gate_out,
    ga_out,
    late_out,
    wf_ref,
    t_ref,
    g_ref,
    far_x,
    far_y,
    near_x,
    near_y,
    early_ref,
    high_ref,
    high_first_ref,
    high_third_ref,
    nm_ref,
    og_ref,
    branch_ref,
    hidden_ref,
    mid_ref,
    send_ref,
    got_ref,
    block_ref,
    wo_ref,
    gate_ref,
    attn_ref,
    ga_ref,
    late_ref,
    scale_ref,
    sum_ref,
    other_sum_ref,
    sends,
    receives,
    locals_,
):
    rows, width = hidden.shape
    quarter = width // 4
    units = wf.shape[1] // n_head
    spans = rows // SPAN
    tiles = 2 * spans
    last = n_head - 1
    place = Place(n_head)
    z, core = place.z, place.core
    place.greet()
    copies = Copies(sends, receives, locals_)
    own, other = pl.ds(0, rows), pl.ds(rows, rows)

    order = (2, 1, 3, 0)
    load_nm = copies.move(nm, nm_ref)
    load_og = copies.move(og, og_ref)
    load_wf = {}
    for slot in order:
        at = pl.ds(slot * units, units)
        lanes = pl.ds(0, width if slot < last else width - quarter)
        load_wf[slot] = copies.move(wf.at[:, at, lanes], wf_ref.at[:, at, lanes])
    early_loads = [
        copies.move(hidden, hidden_ref),
        copies.move(wo, wo_ref),
        copies.move(scale, scale_ref),
        copies.move(attn, attn_ref),
        copies.move(pre.at[:, :, pl.ds(3 * HEAD_DIM, HEAD_DIM)], gate_ref),
    ]
    place.meet()

    def tile(i):
        return pl.ds(pl.multiple_of(i * SPAN, SPAN), SPAN)

    def dot_last(left, right):
        return lax.dot_general(left, right, (((1,), (1,)), ((), ())), preferred_element_type=F32)

    def dot_first(left, right):
        return lax.dot_general(left, right, (((0,), (0,)), ((), ())), preferred_element_type=F32)

    early_slot, down = 1, 2

    def items(slot):
        return down if slot == early_slot else 3

    def g_view(slot, q, half):
        size = units if half is None else units // 2
        start = slot * units + (half or 0) * size
        return g_ref.at[pl.ds(0, items(slot)), pl.ds(start, size), pl.ds(q * quarter, quarter)]

    def late_view(ref, q, half):
        rows_at = pl.ds(last * units + half * (units // 2), units // 2)
        return ref.at[:, rows_at, pl.ds(q * quarter, quarter)]

    base = PER_SCATTER
    late_low, late_high = late_view(wf_ref, 3, 0), late_view(wf_ref, 3, 1)
    copies.send(late_view(wf, 1, 0), late_low, base, base, place.by_y)
    copies.send(late_view(wf, 2, 1), late_high, base + 1, base + 1, place.by_x)
    feed = Scatter(place, copies, g_view, far_x, far_y, near_x, near_y, None, 0, items)
    up_base = base + 2

    def feed_products(slot):
        at = pl.ds(slot * units, units)
        load_wf[slot].wait()

        @pl.loop(0, tiles)
        def _(i):
            rows_at = tile(i)
            left = dot_last(wf_ref[0, at, :], nm_ref[rows_at, :])
            right = dot_last(wf_ref[1, at, :], nm_ref[rows_at, :])
            grad = dot_last(wf_ref[2, at, :], og_ref[rows_at, :])
            t_ref[0, at, rows_at] = (grad * right).astype(BF)
            t_ref[1, at, rows_at] = (grad * left).astype(BF)
            t_ref[2, at, rows_at] = (left * right).astype(BF)

    def feed_gradients(slot):
        at = pl.ds(slot * units, units)

        def gradient(columns, of=(0, 1, 2)):
            for m in of:
                right = og_ref if m == down else nm_ref
                g_ref[m, at, columns] = dot(t_ref[m, at, :], right[:, columns]).astype(BF)

        def gradients(n, of=(0, 1, 2)):
            @pl.loop(0, n)
            def _(q):
                gradient(pl.ds(pl.multiple_of(q * quarter, quarter), quarter), of)

        if slot == 0:
            gradients(4)
            return
        of = tuple(range(items(slot)))
        if slot == early_slot:
            gradients(4, (down,))
            copies.send(g_ref.at[down, at], early_ref, up_base, up_base, place.above(slot))
        gradient(pl.ds(3 * quarter, quarter), of)
        feed.begin(slot)
        gradients(3, of)

    load_nm.wait()
    load_og.wait()
    for slot in order[:2]:
        feed_products(slot)
        feed_gradients(slot)
    feed.middle(order[0])
    copies.receive(late_low, base, place.by_y)
    copies.receive(late_high, base + 1, place.by_x)
    feed_products(order[2])
    feed_gradients(order[2])
    feed_products(order[3])
    feed.middle(order[1])
    base += 2 + 4
    for load in early_loads:
        load.wait()

    @pl.loop(0, spans)
    def _(i):
        at = tile(spans + i)
        total = dot_first(t_ref[0, :, at], wf_ref[0]) + dot_first(t_ref[1, :, at], wf_ref[1])
        send_ref[tile(i), :] = total.astype(BF)

    copies.send(send_ref, got_ref, base, base, place.across)

    @pl.loop(0, spans)
    def _(i):
        at = tile(i)
        total = dot_first(t_ref[0, :, at], wf_ref[0]) + dot_first(t_ref[1, :, at], wf_ref[1])
        mid_ref[at, :] = total

    feed.end(order[0], False)
    both, second_at = pl.ds(0, down), pl.ds(order[0] * units, units)
    near = pl.ds(0, quarter)
    above = place.above(order[0])
    copies.send(g_ref.at[:, second_at, near], high_ref, up_base + 1, up_base + 1, above)
    copies.receive(got_ref, base, place.across)

    @pl.loop(0, rows // 128)
    def _(i):
        at = pl.ds(pl.multiple_of(i * 128, 128), 128)
        grad = mid_ref[at, :] + got_ref[at, :].astype(F32)
        values = hidden_ref[at, :]
        norm = lax.rsqrt(jnp.mean(values * values, axis=-1, keepdims=True) + EPSILON)
        normed = values * norm
        mean = jnp.mean(grad * normed, axis=-1, keepdims=True)
        grad = og_ref[at, :].astype(F32) + norm * (grad - normed * mean)
        mid_ref[at, :] = grad
        branch_ref[at, :] = grad.astype(BF)

    copies.send(branch_ref.at[own], branch_ref.at[other], base + 1, base + 1, place.across)
    copies.move(mid_ref, hidden_grad_out, later=True)
    feed_gradients(order[3])
    copies.receive(early_ref, up_base, place.up)
    add_to(g_ref.at[down, pl.ds(0, units)], early_ref)
    feed.begin(0)
    query_loads = []
    for slot in range(n_head):
        lanes = pl.ds(slot * 2 * HEAD_DIM, 2 * HEAD_DIM)
        query_loads.append(copies.move(query.at[slot], t_ref.at[0, pl.ds(0, 2 * rows), lanes]))

    def gate_back(seq):
        for n in range(spans):
            at = pl.ds(seq * rows + n * SPAN, SPAN)
            grad = dot_last(branch_ref[at, :], wo_ref[...])
            norm = scale_ref[at, :]
            total = jnp.zeros((SPAN, 1), F32)
            for slot in range(n_head):
                lanes = pl.ds(slot * HEAD_DIM, HEAD_DIM)
                part = grad[:, slot * HEAD_DIM : (slot + 1) * HEAD_DIM]
                normed = attn_ref[slot, at, :] * norm
                og_ref[at, lanes] = (part * normed).astype(BF)
                part = part * gate_ref[slot, at, :]
                gate_ref[slot, at, :] = part
                total += jnp.sum(part * normed, axis=-1, keepdims=True)
            sum_ref[at, :] = jnp.broadcast_to(total, (SPAN, HEAD_DIM))

    gate_back(0)
    base += 2
    copies.send(sum_ref.at[own], other_sum_ref.at[other], base, base, place.across)
    copies.receive(branch_ref.at[other], base - 1, place.across)
    copies.move(branch_ref, branch_out, later=True)
    gate_back(1)
    copies.send(sum_ref.at[other], other_sum_ref.at[own], base + 1, base + 1, place.across)
    copies.move(og_ref.at[:, pl.ds(0, n_head * HEAD_DIM)], gate_out, later=True)
    copies.sent(base - 2)
    feed.middle(order[2])

    @pl.loop(0, spans)
    def _(i):
        send_ref[tile(i), :] = dot_first(t_ref[2, :, tile(spans + i)], wf_ref[2]).astype(BF)

    copies.send(send_ref, got_ref, base + 2, base + 2, place.across)

    @pl.loop(0, spans)
    def _(i):
        at = tile(i)
        hidden_ref[at, :] += dot_first(t_ref[2, :, at], wf_ref[2])

    feed.end(order[1], False)
    src = g_ref.at[both, pl.ds(order[1] * units, units), near]
    copies.send(src, high_first_ref, up_base + 2, up_base + 2, place.above(order[1]))
    for load in query_loads:
        load.wait()
    copies.receive(other_sum_ref.at[other], base, place.across)
    copies.receive(other_sum_ref.at[own], base + 1, place.across)

    for slot in range(n_head):
        decay = decay_of(2 * lax.rem(z + slot, n_head) + core)
        early = jnp.exp(-decay * (iota((SPAN, HEAD_DIM), 0) + 1.0))

        @pl.loop(0, tiles)
        def _(i):
            at = tile(i)
            norm = scale_ref[at, :]
            mean = (sum_ref[at, :] + other_sum_ref[at, :]) / width
            grad = norm * (gate_ref[slot, at, :] - attn_ref[slot, at, :] * norm * mean)
            grad = grad.astype(BF)
            ga_ref[slot, at, :] = grad
            q = t_ref[0, at, pl.ds(slot * 2 * HEAD_DIM, 2 * HEAD_DIM)]
            both_terms = dot_first(
                q, jnp.concatenate(split(grad.astype(F32) * early), axis=1)
            )
            late_ref[slot, i] = both_terms[:, :HEAD_DIM] + both_terms[:, HEAD_DIM:]

        copies.move(ga_ref.at[slot], ga_out.at[slot], later=True)
        copies.move(late_ref.at[slot], late_out.at[slot], later=True)

    feed.middle(order[3])
    copies.receive(got_ref, base + 2, place.across)

    @pl.loop(0, rows // 128)
    def _(i):
        at = pl.ds(pl.multiple_of(i * 128, 128), 128)
        block_ref[at, :] = (hidden_ref[at, :] + got_ref[at, :].astype(F32)).astype(BF)

    for q in range(4):
        far = pl.ds(pl.multiple_of(place.at[q] * quarter, quarter), quarter)
        src = block_ref.at[:, pl.ds(q * quarter, quarter)]
        copies.move(src, block_out.at[:, far], later=True)
    feed.end(order[2], False)
    src = g_ref.at[:, pl.ds(order[2] * units, units), near]
    copies.send(src, high_third_ref, up_base + 3, up_base + 3, place.above(order[2]))
    copies.receive(high_ref, up_base + 1, place.up)
    copies.receive(high_first_ref, up_base + 2, place.up)
    feed.end(order[3], False)
    first_rows = pl.ds(0, units)
    add_to(g_ref.at[both, first_rows, near], high_ref.at[both], high_first_ref)
    add_to(g_ref.at[down, first_rows, near], high_ref.at[down])
    copies.receive(high_third_ref, up_base + 3, place.up)
    add_to(g_view(0, 0, None), high_third_ref)
    copies.move(g_view(0, 0, None), feed_out, later=True)
    copies.finish()


def middle(n_head, wf, nm, og, hidden, wo, pre, query, attn, scale):
    rows, width = hidden.shape
    units = wf.shape[1] // n_head
    quarter = width // 4
    tall = 2 * rows
    halves = (n_head, 3, units // 2, quarter)
    wholes = (n_head, 3, units, quarter)
    late = ((n_head, tall // SPAN, 2 * HEAD_DIM, HEAD_DIM), F32)
    buffers = [
        (wf.shape, BF),
        (wf.shape, BF),
        (wf.shape, BF),
        (halves, BF),
        (halves, BF),
        (wholes, BF),
        (wholes, BF),
        ((units, width), BF),
        (wholes[1:], BF),
        ((2, units, quarter), BF),
        (wholes[1:], BF),
        ((tall, width), BF),
        ((tall, width), BF),
        ((tall, width), BF),
        ((rows, width), F32),
        ((rows, width), F32),
        ((rows, width), BF),
        ((rows, width), BF),
        ((rows, width), BF),
        (wo.shape, BF),
        (attn.shape, F32),
        (attn.shape, F32),
        (attn.shape, BF),
        late,
        (scale.shape, F32),
        (scale.shape, F32),
        (scale.shape, F32),
    ]
    outs = [
        (wholes[1:], BF),
        ((rows, width), BF),
        ((rows, width), F32),
        ((tall, width), BF),
        ((tall, n_head * HEAD_DIM), BF),
        (attn.shape, BF),
        late,
    ]
    n_sems = PER_SCATTER + 2 + 4 + 2 + 3
    return pl.pallas_call(
        functools.partial(middle_kernel, n_head),
        out_shape=[jax.ShapeDtypeStruct(*out) for out in outs],
        in_specs=[ANY] * 9,
        out_specs=[ANY] * len(outs),
        scratch_shapes=[pltpu.VMEM(*b) for b in buffers]
        + [
            pltpu.SemaphoreType.DMA((n_sems,)),
            pltpu.SemaphoreType.DMA((n_sems,)),
            pltpu.SemaphoreType.DMA((64,)),
        ],
        compiler_params=pltpu.CompilerParams(
            collective_id=1, has_side_effects=True, vmem_limit_bytes=63 << 20
        ),
        name="middle",
    )(wf, nm, og, hidden, wo, pre, query, attn, scale)


class Share:
    def __init__(self, place, copies, view, base):
        self.place, self.copies, self.view, self.base = place, copies, view, base

    def pass_on(self, q, half, at, device):
        part = self.view(0, q, half)
        self.copies.send(part, part, self.base + at, self.base + at, device)

    def begin(self):
        self.pass_on(0, None, 0, self.place.by_x)
        self.pass_on(0, None, 1, self.place.by_y)
        self.pass_on(0, None, 4, self.place.across)

    def spread(self):
        place, copies, at = self.place, self.copies, self.base
        copies.receive(self.view(0, 1, None), at, place.by_x)
        self.pass_on(1, 0, 2, place.by_y)
        copies.receive(self.view(0, 2, None), at + 1, place.by_y)
        self.pass_on(2, 1, 3, place.by_x)
        self.pass_on(1, None, 5, place.across)
        self.pass_on(2, None, 6, place.across)

    def complete(self):
        place, copies, at = self.place, self.copies, self.base
        copies.receive(self.view(0, 3, 0), at + 2, place.by_y)
        copies.receive(self.view(0, 3, 1), at + 3, place.by_x)
        self.pass_on(3, None, 7, place.across)

    def other_side(self):
        for q in range(4):
            self.copies.receive(self.view(1, q, None), self.base + 4 + q, self.place.across)


PER_SHARE = 8


def last_kernel(
    n_head,
    late,
    feed_piece,
    nin,
    gate_pre,
    gated,
    branch,
    query,
    keys,
    values,
    grad_attn,
    carry,
    fresh,
    pre,
    cosines,
    sines,
    wa,
    hidden_grad,
    block,
    tokens,
    input_ref,
    block_ref,
    feed_ref,
    attn_ref,
    rates_both,
    ga_ref,
    a_far_x,
    a_far_y,
    a_near_x,
    a_near_y,
    a_high,
    g_far_x,
    g_far_y,
    g_near_x,
    g_near_y,
    g_high,
    late_ref,
    pending_ref,
    message_ref,
    nin_ref,
    gate_ref,
    gated_ref,
    branch_ref,
    q_ref,
    k_ref,
    v_ref,
    grad_attn_ref,
    carry_ref,
    fresh_ref,
    qk_pre_ref,
    cos_ref,
    sin_ref,
    pre_ref,
    wa_ref,
    x_ref,
    grad_ref,
    send_ref,
    got_ref,
    rates_ref,
    rates_high,
    rates_sum,
    rates_got,
    sends,
    receives,
    locals_,
):
    rows, width = tokens.shape
    quarter = width // 4
    units = feed_piece.shape[1]
    spans = rows // SPAN
    tiles = 2 * spans
    last = n_head - 1
    three = 3 * HEAD_DIM
    place = Place(n_head)
    place.greet()
    z, core = place.z, place.core
    copies = Copies(sends, receives, locals_)
    order = (2, 1, 3, 0)
    sides = (core, 1 - core)

    own_block = pl.ds(pl.multiple_of(place.plane * quarter, quarter), quarter)
    load_feed = copies.move(feed_piece, feed_ref.at[sides[0], :, :, own_block])
    load_late = copies.move(late, late_ref)
    load_first = [copies.move(nin, nin_ref), copies.move(gate_pre, gate_ref)]
    load_second = [copies.move(gated, gated_ref), copies.move(branch, branch_ref)]
    load_back = [
        copies.move(src, dst)
        for src, dst in (
            (query, q_ref),
            (keys, k_ref),
            (values, v_ref),
            (grad_attn, grad_attn_ref),
            (carry, carry_ref),
        )
    ]
    for seq in range(2):
        for slot in range(n_head):
            load_back.append(copies.move(fresh.at[slot, seq * spans], fresh_ref.at[slot, seq]))

    def slot_load(slot, turn):
        return [
            copies.move(pre.at[slot, :, pl.ds(0, 2 * HEAD_DIM)], qk_pre_ref.at[turn]),
            copies.move(cosines.at[slot], cos_ref.at[turn]),
            copies.move(sines.at[slot], sin_ref.at[turn]),
        ]

    slot_loads = [slot_load(slot, turn) for turn, slot in enumerate(order[:2])]
    late_loads = [
        copies.move(wa, wa_ref),
        copies.move(hidden_grad, grad_ref),
        copies.move(block, block_ref),
    ]
    for q in range(4):
        far = pl.ds(pl.multiple_of(place.at[q] * quarter, quarter), quarter)
        late_loads.append(copies.move(tokens.at[:, far], x_ref.at[:, pl.ds(q * quarter, quarter)]))
    place.meet()

    def tile(i):
        return pl.ds(pl.multiple_of(i * SPAN, SPAN), SPAN)

    def dot_last(left, right):
        return lax.dot_general(left, right, (((1,), (1,)), ((), ())), preferred_element_type=F32)

    def dot_first(left, right):
        return lax.dot_general(left, right, (((0,), (0,)), ((), ())), preferred_element_type=F32)

    def part(start, half, size):
        if half is None:
            return pl.ds(start, size)
        return pl.ds(start + half * (size // 2), size // 2)

    def start_of(q):
        return pl.multiple_of(place.at[q] * quarter, quarter)

    def feed_view(side, q, half):
        return feed_ref.at[sides[side], :, part(0, half, units), pl.ds(start_of(q), quarter)]

    def lanes_view(lanes, side, q, half):
        at = part(0, half, quarter)
        start = pl.multiple_of(start_of(q) + at.start, quarter // 2)
        return attn_ref.at[sides[side], pl.ds(start, at.size), lanes]

    def ga_view(lanes, slot, q, half):
        return ga_ref.at[slot, part(q * quarter, half, quarter), lanes]

    gate_lanes, rest_lanes = pl.ds(three, 2 * HEAD_DIM), pl.ds(0, three)
    weight_lanes = pl.ds(three, HEAD_DIM)
    of_gate = functools.partial(ga_view, gate_lanes)
    of_rest = functools.partial(ga_view, rest_lanes)
    gate = Scatter(place, copies, of_gate, g_far_x, g_far_y, g_near_x, g_near_y, g_high, 0)
    base = PER_SCATTER
    rest = Scatter(place, copies, of_rest, a_far_x, a_far_y, a_near_x, a_near_y, a_high, base)
    base += PER_SCATTER
    to_gate = functools.partial(lanes_view, gate_lanes)
    to_rest = functools.partial(lanes_view, rest_lanes)
    shares = []
    for view in (feed_view, to_gate, to_rest):
        shares.append(Share(place, copies, view, base))
        base += PER_SHARE
    feed_share, gate_share, rest_share = shares

    load_feed.wait()
    feed_share.begin()

    n_chain = 2 * n_head
    chain_base = base
    base += n_chain

    def chain_at(index):
        group, seq = lax.div(index, 2), lax.rem(index, 2)
        return lax.rem(group - z + n_head, n_head), seq, decay_of(2 * group + core)

    def chain_copy(index, slot, seq):
        return pltpu.make_async_remote_copy(
            src_ref=message_ref.at[slot, seq],
            dst_ref=pending_ref.at[lax.rem(slot + 1, n_head), seq],
            send_sem=sends.at[chain_base + index],
            recv_sem=receives.at[chain_base + index],
            device_id=place.down,
            device_id_type=MESH,
        )

    def hand_on(index):
        slot, seq, decay = chain_at(index)
        total = jnp.exp(-decay * rows) * pending_ref[slot, seq].astype(F32)
        for n in range(spans):
            total += jnp.exp(-decay * (n * SPAN)) * late_ref[slot, seq * spans + n]
        message_ref[slot, seq] = total.astype(BF)
        chain_copy(index, slot, seq).start()

    def take(index):
        slot, seq, _ = chain_at(index)
        copies.receive(pending_ref.at[slot, seq], chain_base + index, place.up)

    load_late.wait()

    @pl.when(z == last)
    def _():
        pending_ref[...] = jnp.zeros_like(pending_ref)
        pl.loop(0, n_chain)(hand_on)

    for load in load_first:
        load.wait()

    for load in load_second:
        load.wait()

    def gate_gradient(at):
        grads = dot_first(nin_ref[:, at], gate_ref[...]).astype(BF)
        outs = dot_first(branch_ref[:, at], gated_ref[...]).astype(BF)
        for slot in range(n_head):
            lanes = slice(slot * HEAD_DIM, (slot + 1) * HEAD_DIM)
            ga_ref[slot, at, pl.ds(three, HEAD_DIM)] = grads[:, lanes]
            ga_ref[slot, at, pl.ds(three + HEAD_DIM, HEAD_DIM)] = outs[:, lanes]

    gate_gradient(pl.ds(3 * quarter, quarter))
    for slot in order:
        gate.begin(slot)
    pl.loop(0, 3)(lambda q: gate_gradient(tile(q)))

    @pl.when(jnp.logical_and(z > 0, z < last))
    def _():
        @pl.loop(0, n_chain)
        def _(index):
            take(index)
            hand_on(index)

    for slot in order:
        gate.middle(slot)
    for load in load_back:
        load.wait()

    @pl.when(z == 0)
    def _():
        pl.loop(0, n_chain)(take)

    offsets = iota((SPAN, SPAN), 0) - iota((SPAN, SPAN), 1)

    def back_slot(slot, turn):
        decay = decay_of(2 * lax.rem(z + slot, n_head) + core)
        mask = jnp.where(offsets >= 0.0, jnp.exp(-decay * jnp.maximum(offsets, 0.0)), 0.0)
        places = iota((SPAN, 1), 0)
        early = jnp.exp(-decay * (places + 1.0))
        late_decay = jnp.exp(-decay * (SPAN - 1.0 - places))
        span_decay = jnp.exp(-decay * SPAN)
        rates_ref[slot] = jnp.zeros((8, HEAD_DIM), F32)

        @pl.loop(0, 2)
        def _(seq):
            for n in range(spans):
                at, here = tile(seq * spans + n), pl.ds(n * SPAN, SPAN)
                state = carry_ref[slot, seq].astype(F32)
                if n == 1:
                    state = span_decay * state + fresh_ref[slot, seq]
                later = pending_ref[slot, seq].astype(F32)
                if n == 0:
                    later = span_decay * later + late_ref[slot, seq * spans + 1]
                q, k, v = q_ref[slot, at, :], k_ref[slot, at, :], v_ref[slot, at, :]
                grad = grad_attn_ref[slot, at, :]
                weights = (dot_last(q, k) * mask).astype(BF)
                scores = (dot_last(grad, v) * mask).astype(BF)
                state_high, state_low = split(state)
                grad_query = dot(scores, k)
                grad_query += early * (dot_last(grad, state_high) + dot_last(grad, state_low))
                later_high, later_low = split(later)
                grad_keys = dot_first(scores, q)
                grad_keys += late_decay * (dot_last(v, later_high) + dot_last(v, later_low))
                both = dot(k, jnp.concatenate([later_high, later_low], axis=1))
                grad_values = dot_first(weights, grad)
                grad_values += late_decay * (both[:, :HEAD_DIM] + both[:, HEAD_DIM:])
                pre_ref[slot, at, pl.ds(2 * HEAD_DIM, HEAD_DIM)] = grad_values.astype(BF)
                cosine, sine = cos_ref[turn, here, :], sin_ref[turn, here, :]
                angles = jnp.zeros((SPAN, HEAD_DIM), F32)
                for i, turned in enumerate((grad_query, grad_keys)):
                    lanes = pl.ds(i * HEAD_DIM, HEAD_DIM)
                    value = qk_pre_ref[turn, at, lanes]
                    by_cos, by_sin = turned[:, :HEAD_DIM], turned[:, HEAD_DIM:]
                    sigmoid = 1.0 / (1.0 + jnp.exp(-value))
                    act = by_cos * cosine + by_sin * sine
                    angles += value * sigmoid * (by_sin * cosine - by_cos * sine)
                    act = act * sigmoid * (1.0 + value * (1.0 - sigmoid))
                    pre_ref[slot, at, lanes] = act.astype(BF)
                steps = (z * rows + n * SPAN).astype(F32) + places
                rates_ref[slot, pl.ds(0, 1), :] += jnp.sum(steps * angles, axis=0, keepdims=True)

    def rest_gradient(slot, at):
        ga_ref[slot, at, rest_lanes] = dot_first(nin_ref[:, at], pre_ref[slot]).astype(BF)

    rates_base = base
    base += n_head + 3
    for i, slot in enumerate(order):
        for load in slot_loads[i]:
            load.wait()
        back_slot(slot, i % 2)
        if i + 2 < n_head:
            slot_loads.append(slot_load(order[i + 2], i % 2))
        if slot:
            at = rates_base + slot
            copies.send(rates_ref.at[slot], rates_high.at[slot - 1], at, at, place.above(slot))
        rest_gradient(slot, pl.ds(3 * quarter, quarter))
        rest.begin(slot)
        pl.loop(0, 3)(lambda q: rest_gradient(slot, tile(q)))
    for slot in order:
        gate.end(slot)
    rest.middle(order[0])
    rest.middle(order[1])
    for load in late_loads:
        load.wait()

    def grad_in(at):
        total = dot_last(gate_ref[at, :], wa_gate())
        for slot in range(n_head):
            total += dot_last(pre_ref[slot, at, :], wa_ref[slot, :, rest_lanes])
        return total

    def wa_gate():
        return jnp.concatenate([wa_ref[slot, :, weight_lanes] for slot in range(n_head)], axis=1)

    @pl.loop(0, spans)
    def _(i):
        send_ref[tile(i), :] = grad_in(tile(spans + i)).astype(BF)

    copies.send(send_ref, got_ref, base, base, place.across)
    rest.middle(order[2])

    total = rates_ref[0]
    for slot in range(1, n_head):
        copies.receive(rates_high.at[slot - 1], rates_base + slot, place.up)
        total += rates_high[slot - 1]
    rates_sum[0] = total
    rates_base += n_head
    copies.send(rates_sum.at[0], rates_got.at[0], rates_base, rates_base, place.by_x)
    rest.middle(order[3])
    feed_share.spread()
    rest.end(order[0])
    copies.receive(rates_got.at[0], rates_base, place.by_x)
    rates_sum[1] = total + rates_got[0]
    copies.send(rates_sum.at[1], rates_got.at[1], rates_base + 1, rates_base + 1, place.by_y)
    copies.receive(got_ref, base, place.across)

    @pl.loop(0, spans)
    def _(i):
        at = tile(i)
        values = x_ref[at, :].astype(F32)
        norm = lax.rsqrt(jnp.mean(values * values, axis=-1, keepdims=True) + EPSILON)
        normed = values * norm
        grad = grad_in(at) + got_ref[at, :].astype(F32)
        mean = jnp.mean(grad * normed, axis=-1, keepdims=True)
        grad_ref[at, :] += norm * (grad - normed * mean)

    for q in range(4):
        src = grad_ref.at[:, pl.ds(q * quarter, quarter)]
        copies.move(src, input_ref.at[:, pl.ds(start_of(q), quarter)], later=True)
    gate.total(to_gate(0, 0, None))
    gate_share.begin()
    rest.end(order[1])
    copies.receive(rates_got.at[1], rates_base + 1, place.by_y)
    rates_both[sides[0]] = rates_sum[1] + rates_got[1]
    mine = rates_both.at[sides[0]]
    copies.send(mine, mine, rates_base + 2, rates_base + 2, place.across)
    feed_share.complete()
    rest.end(order[2])
    rest.end(order[3])
    rest.total(to_rest(0, 0, None))
    rest_share.begin()
    gate_share.spread()
    copies.receive(rates_both.at[sides[1]], rates_base + 2, place.across)
    feed_share.other_side()
    rest_share.spread()
    gate_share.complete()
    rest_share.complete()
    for share in shares[1:]:
        share.other_side()

    @pl.when(z > 0)
    def _():
        @pl.loop(0, n_chain)
        def _(index):
            slot, seq, _ = chain_at(index)
            chain_copy(index, slot, seq).wait_send()

    copies.finish()


def last(
    n_head,
    late,
    feed_piece,
    nin,
    gate_pre,
    gated,
    branch,
    query,
    keys,
    values,
    grad_attn,
    carry,
    fresh,
    pre,
    cosines,
    sines,
    wa,
    hidden_grad,
    block,
    tokens,
):
    rows, width = tokens.shape
    _, units, quarter = feed_piece.shape
    tall = 2 * rows

    def scatter_buffers(shape, halved):
        half = tuple(n // 2 if i == halved else n for i, n in enumerate(shape))
        return [
            ((n_head,) + half, BF),
            ((n_head,) + half, BF),
            ((n_head,) + shape, BF),
            ((n_head,) + shape, BF),
            ((n_head - 1,) + shape, BF),
        ]

    outs = [
        ((rows, width), F32),
        ((rows, width), BF),
        ((2, 3, units, width), BF),
        ((2, width, 5 * HEAD_DIM), BF),
        ((2, 8, HEAD_DIM), F32),
    ]
    chain = ((n_head, 2, 2 * HEAD_DIM, HEAD_DIM), BF)
    buffers = [
        ((n_head, width, 5 * HEAD_DIM), BF),
        *scatter_buffers((quarter, 3 * HEAD_DIM), 0),
        *scatter_buffers((quarter, 2 * HEAD_DIM), 0),
        (late.shape, F32),
        chain,
        chain,
        (nin.shape, BF),
        (gate_pre.shape, BF),
        (gated.shape, BF),
        (branch.shape, BF),
        (query.shape, BF),
        (keys.shape, BF),
        (values.shape, BF),
        (grad_attn.shape, BF),
        chain,
        (chain[0], F32),
        ((2, tall, 2 * HEAD_DIM), F32),
        ((2, rows, HEAD_DIM), F32),
        ((2, rows, HEAD_DIM), F32),
        ((n_head, tall, 3 * HEAD_DIM), BF),
        (wa.shape, BF),
        ((rows, width), BF),
        ((rows, width), F32),
        ((rows, width), BF),
        ((rows, width), BF),
        ((n_head, 8, HEAD_DIM), F32),
        ((n_head - 1, 8, HEAD_DIM), F32),
        ((2, 8, HEAD_DIM), F32),
        ((2, 8, HEAD_DIM), F32),
    ]
    n_sems = 2 * PER_SCATTER + 3 * PER_SHARE + 2 * n_head + n_head + 3 + 1
    arrays = [late, feed_piece, nin, gate_pre, gated, branch, query, keys, values, grad_attn]
    arrays += [carry, fresh, pre, cosines, sines, wa, hidden_grad, block, tokens]
    arrays = [pltpu.with_memory_space_constraint(array, pltpu.HBM) for array in arrays]
    return pl.pallas_call(
        functools.partial(last_kernel, n_head),
        out_shape=[pltpu.VMEM(*out) for out in outs],
        in_specs=[ANY] * len(arrays),
        out_specs=[IN_VMEM] * len(outs),
        scratch_shapes=[pltpu.VMEM(*b) for b in buffers]
        + [
            pltpu.SemaphoreType.DMA((n_sems,)),
            pltpu.SemaphoreType.DMA((n_sems,)),
            pltpu.SemaphoreType.DMA((64,)),
        ],
        compiler_params=pltpu.CompilerParams(
            collective_id=2, has_side_effects=True, vmem_limit_bytes=52 << 20
        ),
        name="last",
    )(*arrays)


def finish_kernel(grad, block, feed, attn, rates, *refs):
    outs, results, locals_ = refs[:11], refs[11:-1], refs[-1]
    copies = Copies(None, None, locals_)
    (block_out, grad_out, q_out, k_out, v_out, g_out, o_out, rates_out, l_out, r_out, d_out) = outs
    units = feed.shape[2]
    copies.move(grad, grad_out, later=True)
    copies.move(block, block_out, later=True)
    l_ref, r_ref, d_ref, q_ref, k_ref, v_ref, g_ref, o_ref, rates_ref = results
    for side in range(2):
        rates_ref[:, pl.ds(side * HEAD_DIM, HEAD_DIM)] = rates[side, pl.ds(0, 1), :]
    copies.move(rates_ref, rates_out, later=True)
    for i, (ref, out) in enumerate(((l_ref, l_out), (r_ref, r_out), (d_ref, d_out))):
        for side in range(2):
            at = pl.ds(side * units, units)
            ref[at, :] = feed[side, i].astype(F32)
            copies.move(ref.at[at], out.at[at], later=True)
    for i, (ref, out) in enumerate(((q_ref, q_out), (k_ref, k_out), (v_ref, v_out), (g_ref, g_out))):
        lanes = pl.ds(i * HEAD_DIM, HEAD_DIM)
        for side in range(2):
            ref[:, pl.ds(side * HEAD_DIM, HEAD_DIM)] = attn[side, :, lanes].astype(F32)
        copies.move(ref, out, later=True)
    for side in range(2):
        lanes = pl.ds(4 * HEAD_DIM, HEAD_DIM)
        o_ref[pl.ds(side * HEAD_DIM, HEAD_DIM), :] = attn[side, :, lanes].T.astype(F32)
    copies.move(o_ref, o_out, later=True)
    copies.finish()


def finish(grad, block, feed, attn, rates):
    _, _, units, width = feed.shape
    projection = ((width, 2 * HEAD_DIM), F32)
    back = ((2 * HEAD_DIM, width), F32)
    results = [((2 * units, width), F32)] * 3 + [projection] * 4 + [back]
    results.append(((1, 2 * HEAD_DIM), F32))
    outs = [(block.shape, BF), (grad.shape, F32)] + results[3:] + results[:3]
    return pl.pallas_call(
        finish_kernel,
        out_shape=[jax.ShapeDtypeStruct(*out) for out in outs],
        in_specs=[IN_VMEM] * 5,
        out_specs=[ANY] * len(outs),
        scratch_shapes=[pltpu.VMEM(*b) for b in results] + [pltpu.SemaphoreType.DMA((48,))],
        compiler_params=pltpu.CompilerParams(vmem_limit_bytes=24 << 20),
        name="finish",
    )(grad, block, feed, attn, rates)


def make(n_dp, n_head):
    def on_device(
        tokens,
        attn_query,
        attn_key,
        attn_value,
        attn_gate,
        attn_out,
        rotation_rates,
        ffn_left,
        ffn_right,
        ffn_down,
        out_grad,
    ):
        rates_in = rotation_rates.reshape(1, -1)
        (
            attn_weights,
            out_w,
            ffn_all,
            gathered_in,
            pre,
            query,
            keys,
            values,
            attn,
            cosines,
            sines,
            fresh,
            carry,
            scale_attn,
            gated,
            hidden,
            gathered_mid,
            grad_rows,
        ) = forward(
            n_head,
            tokens,
            out_grad,
            attn_query,
            attn_key,
            attn_value,
            attn_gate,
            attn_out,
            ffn_left.T,
            ffn_right.T,
            ffn_down,
            rates_in,
        )
        feed_piece, block_out, grad_hidden, branch_rows, gate_pre, grad_attn, late = middle(
            n_head,
            ffn_all,
            gathered_mid,
            grad_rows,
            hidden,
            out_w,
            pre,
            query,
            attn,
            scale_attn,
        )
        grads = last(
            n_head,
            late,
            feed_piece,
            gathered_in,
            gate_pre,
            gated,
            branch_rows,
            query,
            keys,
            values,
            grad_attn,
            carry,
            fresh,
            pre,
            cosines,
            sines,
            attn_weights,
            grad_hidden,
            block_out,
            tokens,
        )
        results = finish(*grads)
        rates_grad, left_grad, right_grad = results[7][0], results[8].T, results[9].T
        results = list(results[:7]) + [rates_grad, left_grad, right_grad, results[10]]
        if n_dp > 8:
            groups = [[i + 8 * j for j in range(n_dp // 8)] for i in range(8)]
            grads = [lax.psum(grad, "dp", axis_index_groups=groups) for grad in results[2:]]
            results = results[:2] + grads
        return tuple(results)

    return on_device


def solution(mesh):
    weights = (P(None, "head"),) * 4 + (P("head", None), P("head")) + (P(None, "head"),) * 2
    weights = weights + (P("head", None),)
    rows = P(("dp", "head"), None)
    return jax.shard_map(
        make(mesh.shape["dp"], mesh.shape["head"]),
        mesh=mesh,
        in_specs=(rows,) + weights + (rows,),
        out_specs=(rows, rows) + weights,
        check_vma=False,
    )
```

profile of v0, /device:TPU:1, one launch (start us, length us, event | category | flops | bytes accessed | tf_op | source)
XLA Modules:
  0.0 270.0 jit_solution(9153380976995112729)
XLA Ops:
  0.6 101.7 %forward.1 = (bf16[4,1024,512]{2,1,0:T(8,128)(2,1)}, bf16[512,1024]{1,0:T(8,128)(2,1)}, bf16[3,1408,1024]{2,1,0:T(8,128)(2,1)}, bf16[1024,1024]{1,0:T(8,128)(2,1...) custom-call(bf16[512,1024]{1,0:T(8,128)(2,1)} %tokens.3, ...), custom_call_target="tpu_custom_call" | custom-call | tf_op jit(solution)/shard_map/forward/pallas_call | solution.py:628
  102.3 80.0 %middle.1 = (bf16[3,352,256]{2,1,0:T(8,128)(2,1)}, bf16[512,1024]{1,0:T(8,128)(2,1)}, f32[512,1024]{1,0:T(8,128)}, bf16[1024,1024]{1,0:T(8,128)(2,1)}, bf16[1024...) custom-call(bf16[3,1408,1024]{2,1,0:T(8,128)(2,1)} %get-tuple-element.52.wf, ...), custom_call_target="tpu_custom_call" | custom-call | tf_op jit(solution)/shard_map/middle/pallas_call | solution.py:1068
  182.3 81.1 %last.1 = (f32[512,1024]{1,0:T(8,128)S(1)}, bf16[512,1024]{1,0:T(8,128)(2,1)S(1)}, bf16[2,3,352,1024]{3,2,1,0:T(8,128)(2,1)S(1)}, bf16[2,1024,640]{2,1,0:T(8,128)(2,1)S(1)}, f32[2,8,128]{2,1,0:T(8,128)S(1)}) custom-call(f32[4,4,256,128]{3,2,1,0:T(8,128)} %get-tuple-element.61.late, bf16[3,352,256]{2,1,0:T(8,128)(2,1)} %get-tuple-element.62.feed_piece, ...), custom_call_target="tpu_custom_call" | custom-call | tf_op jit(solution)/shard_map/last/pallas_call | solution.py:1586
  263.5 6.4 %finish.1 = (bf16[512,1024]{1,0:T(8,128)(2,1)}, f32[512,1024]{1,0:T(8,128)}, f32[1024,256]{1,0:T(8,128)}, f32[1024,256]{1,0:T(8,128)}, f32[1024,256]{1,0:T(8,128...) custom-call(f32[512,1024]{1,0:T(8,128)S(1)} %get-tuple-element.77.gr, ...), custom_call_target="tpu_custom_call" | custom-call | tf_op jit(solution)/shard_map/finish/pallas_call | solution.py:1639
where the time goes:
time: 275 us; the launch traced here: 270 us
  Pallas kernels  269 us (98%)
    pallas_call x1, Pallas kernels, forward(): pl.pallas_call(functools.partial(forward_kernel, n_head), out_shape=[jax....  102 us
    pallas_call x1, Pallas kernels, last(): pl.pallas_call(functools.partial(last_kernel, n_head), out_shape=[pltpu.V...  81.1 us
    pallas_call x1, Pallas kernels, middle(): pl.pallas_call(functools.partial(middle_kernel, n_head), out_shape=[jax.S...  80 us
    pallas_call x1, Pallas kernels, finish(): pl.pallas_call(finish_kernel, out_shape=[jax.ShapeDtypeStruct(*out) for o...  6.35 us

commit v1 on v0

--- a/solution.py
+++ b/solution.py
@@ -1422,29 +1422,6 @@
         rest_gradient(slot, pl.ds(3 * quarter, quarter))
         rest.begin(slot)
         pl.loop(0, 3)(lambda q: rest_gradient(slot, tile(q)))
-    for slot in order:
-        gate.end(slot)
-    rest.middle(order[0])
-    rest.middle(order[1])
-    for load in late_loads:
-        load.wait()
-
-    def grad_in(at):
-        total = dot_last(gate_ref[at, :], wa_gate())
-        for slot in range(n_head):
-            total += dot_last(pre_ref[slot, at, :], wa_ref[slot, :, rest_lanes])
-        return total
-
-    def wa_gate():
-        return jnp.concatenate([wa_ref[slot, :, weight_lanes] for slot in range(n_head)], axis=1)
-
-    @pl.loop(0, spans)
-    def _(i):
-        send_ref[tile(i), :] = grad_in(tile(spans + i)).astype(BF)
-
-    copies.send(send_ref, got_ref, base, base, place.across)
-    rest.middle(order[2])
-
     total = rates_ref[0]
     for slot in range(1, n_head):
         copies.receive(rates_high.at[slot - 1], rates_base + slot, place.up)
@@ -1452,12 +1429,35 @@
     rates_sum[0] = total
     rates_base += n_head
     copies.send(rates_sum.at[0], rates_got.at[0], rates_base, rates_base, place.by_x)
+    for slot in order:
+        gate.end(slot)
+    copies.receive(rates_got.at[0], rates_base, place.by_x)
+    rates_sum[1] = total + rates_got[0]
+    copies.send(rates_sum.at[1], rates_got.at[1], rates_base + 1, rates_base + 1, place.by_y)
+    rest.middle(order[0])
+    rest.middle(order[1])
+    for load in late_loads:
+        load.wait()
+
+    def grad_in(at):
+        total = dot_last(gate_ref[at, :], wa_gate())
+        for slot in range(n_head):
+            total += dot_last(pre_ref[slot, at, :], wa_ref[slot, :, rest_lanes])
+        return total
+
+    def wa_gate():
+        return jnp.concatenate([wa_ref[slot, :, weight_lanes] for slot in range(n_head)], axis=1)
+
+    @pl.loop(0, spans)
+    def _(i):
+        send_ref[tile(i), :] = grad_in(tile(spans + i)).astype(BF)
+
+    copies.send(send_ref, got_ref, base, base, place.across)
+    rest.middle(order[2])
+
     rest.middle(order[3])
     feed_share.spread()
     rest.end(order[0])
-    copies.receive(rates_got.at[0], rates_base, place.by_x)
-    rates_sum[1] = total + rates_got[0]
-    copies.send(rates_sum.at[1], rates_got.at[1], rates_base + 1, rates_base + 1, place.by_y)
     copies.receive(got_ref, base, place.across)
 
     @pl.loop(0, spans)
@@ -1476,15 +1476,15 @@
     gate.total(to_gate(0, 0, None))
     gate_share.begin()
     rest.end(order[1])
+    rest.end(order[2])
+    rest.end(order[3])
+    rest.total(to_rest(0, 0, None))
+    rest_share.begin()
     copies.receive(rates_got.at[1], rates_base + 1, place.by_y)
     rates_both[sides[0]] = rates_sum[1] + rates_got[1]
     mine = rates_both.at[sides[0]]
     copies.send(mine, mine, rates_base + 2, rates_base + 2, place.across)
     feed_share.complete()
-    rest.end(order[2])
-    rest.end(order[3])
-    rest.total(to_rest(0, 0, None))
-    rest_share.begin()
     gate_share.spread()
     copies.receive(rates_both.at[sides[1]], rates_base + 2, place.across)
     feed_share.other_side()

time: 275 us -> 273 us (level)
  no operation moved by 1% of the time
where the time goes in v1:
time: 273 us; the launch traced here: 268 us
  Pallas kernels  267 us (98%)
    pallas_call x1, Pallas kernels, forward(): pl.pallas_call(functools.partial(forward_kernel, n_head), out_shape=[jax....  102 us
    pallas_call x1, Pallas kernels, middle(): pl.pallas_call(functools.partial(middle_kernel, n_head), out_shape=[jax.S...  80 us
    pallas_call x1, Pallas kernels, last(): pl.pallas_call(functools.partial(last_kernel, n_head), out_shape=[pltpu.V...  78.9 us
    pallas_call x1, Pallas kernels, finish(): pl.pallas_call(finish_kernel, out_shape=[jax.ShapeDtypeStruct(*out) for o...  6.35 us

profile of v1, /device:TPU:1, one launch (start us, length us, event | category | flops | bytes accessed | tf_op | source)
XLA Modules:
  0.0 267.8 jit_solution(2537874822843026483)
XLA Ops:
  0.6 101.7 %forward.1 = (bf16[4,1024,512]{2,1,0:T(8,128)(2,1)}, bf16[512,1024]{1,0:T(8,128)(2,1)}, bf16[3,1408,1024]{2,1,0:T(8,128)(2,1)}, bf16[1024,1024]{1,0:T(8,128)(2,1...) custom-call(bf16[512,1024]{1,0:T(8,128)(2,1)} %tokens.3, ...), custom_call_target="tpu_custom_call" | custom-call | tf_op jit(solution)/shard_map/forward/pallas_call | solution.py:628
  102.3 80.0 %middle.1 = (bf16[3,352,256]{2,1,0:T(8,128)(2,1)}, bf16[512,1024]{1,0:T(8,128)(2,1)}, f32[512,1024]{1,0:T(8,128)}, bf16[1024,1024]{1,0:T(8,128)(2,1)}, bf16[1024...) custom-call(bf16[3,1408,1024]{2,1,0:T(8,128)(2,1)} %get-tuple-element.52.wf, ...), custom_call_target="tpu_custom_call" | custom-call | tf_op jit(solution)/shard_map/middle/pallas_call | solution.py:1068
  182.3 78.9 %last.1 = (f32[512,1024]{1,0:T(8,128)S(1)}, bf16[512,1024]{1,0:T(8,128)(2,1)S(1)}, bf16[2,3,352,1024]{3,2,1,0:T(8,128)(2,1)S(1)}, bf16[2,1024,640]{2,1,0:T(8,128)(2,1)S(1)}, f32[2,8,128]{2,1,0:T(8,128)S(1)}) custom-call(f32[4,4,256,128]{3,2,1,0:T(8,128)} %get-tuple-element.61.late, bf16[3,352,256]{2,1,0:T(8,128)(2,1)} %get-tuple-element.62.feed_piece, ...), custom_call_target="tpu_custom_call" | custom-call | tf_op jit(solution)/shard_map/last/pallas_call | solution.py:1586
  261.3 6.4 %finish.1 = (bf16[512,1024]{1,0:T(8,128)(2,1)}, f32[512,1024]{1,0:T(8,128)}, f32[1024,256]{1,0:T(8,128)}, f32[1024,256]{1,0:T(8,128)}, f32[1024,256]{1,0:T(8,128...) custom-call(f32[512,1024]{1,0:T(8,128)S(1)} %get-tuple-element.77.gr, ...), custom_call_target="tpu_custom_call" | custom-call | tf_op jit(solution)/shard_map/finish/pallas_call | solution.py:1639

commit v2 on v1

--- a/solution.py
+++ b/solution.py
@@ -299,6 +299,8 @@
     attn_all.append(Gather(place, copies, wo_view, 2 * PER_GATHER))
     feed = Gather(place, copies, wf_view, 3 * PER_GATHER, late=last)
     base = 4 * PER_GATHER
+    for step in range(1, n_head):
+        copies.send(rates, rates_ref.at[step], base + step, base + step, place.below(step))
     for loads, part in zip((own_loads[0][:2], own_loads[0][2:4], own_loads[0][4:5]), attn_all):
         for load in loads:
             load.wait()
@@ -311,8 +313,6 @@
         for q in range(4)
     ]
     own_loads += [own_weights(q) for q in range(1, 4)]
-    for step in range(1, n_head):
-        copies.send(rates, rates_ref.at[step], base + step, base + step, place.below(step))
     rates_ref[0] = rates[...]
 
     for load in token_loads:
@@ -327,14 +327,21 @@
         at = pl.ds(pl.multiple_of(i * 128, 128), 128)
         nin_ref[at, :] = norm_rows(x_ref[at, :].astype(F32)).astype(BF)
 
-    base += 4
+    base += 5
+    nin_other = nin_ref.at[pl.ds(rows, rows)]
+    copies.send(nin_ref.at[pl.ds(0, rows)], nin_other, base, base, place.across)
+    inner = jnp.logical_and(z > 0, z < last)
+    first = 1 + 2 * lax.div(z, last)
+    second = 2 + lax.rem(lax.div(z + 1, 2), 2)
+    third = 6 - first - second
+    for part in attn_all:
+        part.arrived(first)
+        part.arrived(second, inner)
     for load in grad_loads:
         load.wait()
     og_other = og_ref.at[pl.ds(rows, rows)]
-    copies.send(og_ref.at[pl.ds(0, rows)], og_other, base, base, place.across)
-    base += 1
-    nin_other = nin_ref.at[pl.ds(rows, rows)]
-    copies.send(nin_ref.at[pl.ds(0, rows)], nin_other, base, base, place.across)
+    og_base = base - 1
+    copies.send(og_ref.at[pl.ds(0, rows)], og_other, og_base, og_base, place.across)
     for q, loads in enumerate(own_loads):
         for load in loads[5:] if q == 0 else loads:
             load.wait()
@@ -344,8 +351,6 @@
     copies.move(nin_ref, nin_out, later=True)
     own_rows = pl.ds(0, units)
     copies.move(wf_ref.at[:, own_rows], wf_out.at[:, own_rows], later=True)
-    copies.receive(og_other, base - 1, place.across)
-    copies.move(og_ref, og_out, later=True)
 
     def decay_of(head):
         exponent = jnp.full((1, 1), -8.0 / HEADS, F32) * (head + 1).astype(F32)
@@ -422,15 +427,9 @@
         ):
             copies.move(ref.at[slot], out.at[slot], later=True)
 
-    first = 1 + 2 * lax.div(z, last)
-    second = 2 + lax.rem(lax.div(z + 1, 2), 2)
-    third = 6 - first - second
-
-    for part in attn_all:
-        part.arrived(first)
     slot_compute(0)
     for part in attn_all:
-        part.arrived(second)
+        part.arrived(second, jnp.logical_not(inner))
     for part in attn_all:
         part.spread(first)
     for part in attn_all:
@@ -447,7 +446,6 @@
     for part in attn_all[:2]:
         part.complete(second)
     slot_compute(second)
-    inner = jnp.logical_and(z > 0, z < last)
     feed.arrived(second, inner)
     for part in attn_all[:2]:
         part.complete(third)
@@ -500,6 +498,8 @@
             pl.when(z < last)(lambda: hand_on(index, slot, seq, decay))
 
     copies.move(carry_ref, carry_out, later=True)
+    copies.receive(og_other, og_base, place.across)
+    copies.move(og_ref, og_out, later=True)
     feed.spread(second)
 
     def feed_done(slot):

time: 273 us -> 270 us (0.989)
  Pallas kernels: 267 us -> 264 us
    pallas_call x1, Pallas kernels: 102 us -> 98.3 us  [forward(): pl.pallas_call(functools.partial(forward_kernel, n_head), out_shape=[jax....]
where the time goes in v2:
time: 270 us; the launch traced here: 264 us
  Pallas kernels  264 us (98%)
    pallas_call x1, Pallas kernels, forward(): pl.pallas_call(functools.partial(forward_kernel, n_head), out_shape=[jax....  98.3 us
    pallas_call x1, Pallas kernels, middle(): pl.pallas_call(functools.partial(middle_kernel, n_head), out_shape=[jax.S...  80 us
    pallas_call x1, Pallas kernels, last(): pl.pallas_call(functools.partial(last_kernel, n_head), out_shape=[pltpu.V...  78.9 us
    pallas_call x1, Pallas kernels, finish(): pl.pallas_call(finish_kernel, out_shape=[jax.ShapeDtypeStruct(*out) for o...  6.35 us

profile of v2, /device:TPU:1, one launch (start us, length us, event | category | flops | bytes accessed | tf_op | source)
XLA Modules:
  0.0 264.4 jit_solution(879610748593383112)
XLA Ops:
  0.6 98.3 %forward.1 = (bf16[4,1024,512]{2,1,0:T(8,128)(2,1)}, bf16[512,1024]{1,0:T(8,128)(2,1)}, bf16[3,1408,1024]{2,1,0:T(8,128)(2,1)}, bf16[1024,1024]{1,0:T(8,128)(2,1...) custom-call(bf16[512,1024]{1,0:T(8,128)(2,1)} %tokens.3, ...), custom_call_target="tpu_custom_call" | custom-call | tf_op jit(solution)/shard_map/forward/pallas_call | solution.py:628
  98.9 80.0 %middle.1 = (bf16[3,352,256]{2,1,0:T(8,128)(2,1)}, bf16[512,1024]{1,0:T(8,128)(2,1)}, f32[512,1024]{1,0:T(8,128)}, bf16[1024,1024]{1,0:T(8,128)(2,1)}, bf16[1024...) custom-call(bf16[3,1408,1024]{2,1,0:T(8,128)(2,1)} %get-tuple-element.52.wf, ...), custom_call_target="tpu_custom_call" | custom-call | tf_op jit(solution)/shard_map/middle/pallas_call | solution.py:1068
  179.0 78.9 %last.1 = (f32[512,1024]{1,0:T(8,128)S(1)}, bf16[512,1024]{1,0:T(8,128)(2,1)S(1)}, bf16[2,3,352,1024]{3,2,1,0:T(8,128)(2,1)S(1)}, bf16[2,1024,640]{2,1,0:T(8,128)(2,1)S(1)}, f32[2,8,128]{2,1,0:T(8,128)S(1)}) custom-call(f32[4,4,256,128]{3,2,1,0:T(8,128)} %get-tuple-element.61.late, bf16[3,352,256]{2,1,0:T(8,128)(2,1)} %get-tuple-element.62.feed_piece, ...), custom_call_target="tpu_custom_call" | custom-call | tf_op jit(solution)/shard_map/last/pallas_call | solution.py:1586
  257.9 6.4 %finish.1 = (bf16[512,1024]{1,0:T(8,128)(2,1)}, f32[512,1024]{1,0:T(8,128)}, f32[1024,256]{1,0:T(8,128)}, f32[1024,256]{1,0:T(8,128)}, f32[1024,256]{1,0:T(8,128...) custom-call(f32[512,1024]{1,0:T(8,128)S(1)} %get-tuple-element.77.gr, ...), custom_call_target="tpu_custom_call" | custom-call | tf_op jit(solution)/shard_map/finish/pallas_call | solution.py:1639

commit v3 on v2

--- a/solution.py
+++ b/solution.py
@@ -503,9 +503,11 @@
     feed.spread(second)
 
     def feed_done(slot):
+        at = pl.ds(pl.multiple_of(slot * units, 16), units)
+        near, far = pl.ds(0, 3 * quarter), pl.ds(3 * quarter, quarter)
+        copies.move(wf_ref.at[:, at, near], wf_out.at[:, at, near], later=True)
         feed.complete(slot)
-        at = pl.ds(pl.multiple_of(slot * units, 16), units)
-        copies.move(wf_ref.at[:, at], wf_out.at[:, at], later=True)
+        copies.move(wf_ref.at[:, at, far], wf_out.at[:, at, far], later=True)
 
     def apply(seq):
         mine = pl.ds(seq * rows, rows)
@@ -634,7 +636,7 @@
         + [
             pltpu.SemaphoreType.DMA((n_sems,)),
             pltpu.SemaphoreType.DMA((n_sems,)),
-            pltpu.SemaphoreType.DMA((96,)),
+            pltpu.SemaphoreType.DMA((112,)),
         ],
         compiler_params=pltpu.CompilerParams(
             collective_id=0, has_side_effects=True, vmem_limit_bytes=62 << 20
@@ -1459,6 +1461,7 @@
     feed_share.spread()
     rest.end(order[0])
     copies.receive(got_ref, base, place.across)
+    rest.end(order[1])
 
     @pl.loop(0, spans)
     def _(i):
@@ -1475,7 +1478,6 @@
         copies.move(src, input_ref.at[:, pl.ds(start_of(q), quarter)], later=True)
     gate.total(to_gate(0, 0, None))
     gate_share.begin()
-    rest.end(order[1])
     rest.end(order[2])
     rest.end(order[3])
     rest.total(to_rest(0, 0, None))

time: 270 us -> 270 us (level)
  no operation moved by 1% of the time
where the time goes in v3:
time: 270 us; the launch traced here: 265 us
  Pallas kernels  264 us (98%)
    pallas_call x1, Pallas kernels, forward(): pl.pallas_call(functools.partial(forward_kernel, n_head), out_shape=[jax....  98.4 us
    pallas_call x1, Pallas kernels, middle(): pl.pallas_call(functools.partial(middle_kernel, n_head), out_shape=[jax.S...  80 us
    pallas_call x1, Pallas kernels, last(): pl.pallas_call(functools.partial(last_kernel, n_head), out_shape=[pltpu.V...  79 us
    pallas_call x1, Pallas kernels, finish(): pl.pallas_call(finish_kernel, out_shape=[jax.ShapeDtypeStruct(*out) for o...  6.35 us

profile of v3, /device:TPU:1, one launch (start us, length us, event | category | flops | bytes accessed | tf_op | source)
XLA Modules:
  0.0 264.6 jit_solution(9914190862916508435)
XLA Ops:
  0.6 98.4 %forward.1 = (bf16[4,1024,512]{2,1,0:T(8,128)(2,1)}, bf16[512,1024]{1,0:T(8,128)(2,1)}, bf16[3,1408,1024]{2,1,0:T(8,128)(2,1)}, bf16[1024,1024]{1,0:T(8,128)(2,1...) custom-call(bf16[512,1024]{1,0:T(8,128)(2,1)} %tokens.3, ...), custom_call_target="tpu_custom_call" | custom-call | tf_op jit(solution)/shard_map/forward/pallas_call | solution.py:630
  99.1 80.0 %middle.1 = (bf16[3,352,256]{2,1,0:T(8,128)(2,1)}, bf16[512,1024]{1,0:T(8,128)(2,1)}, f32[512,1024]{1,0:T(8,128)}, bf16[1024,1024]{1,0:T(8,128)(2,1)}, bf16[1024...) custom-call(bf16[3,1408,1024]{2,1,0:T(8,128)(2,1)} %get-tuple-element.52.wf, ...), custom_call_target="tpu_custom_call" | custom-call | tf_op jit(solution)/shard_map/middle/pallas_call | solution.py:1070
  179.0 79.0 %last.1 = (f32[512,1024]{1,0:T(8,128)S(1)}, bf16[512,1024]{1,0:T(8,128)(2,1)S(1)}, bf16[2,3,352,1024]{3,2,1,0:T(8,128)(2,1)S(1)}, bf16[2,1024,640]{2,1,0:T(8,128)(2,1)S(1)}, f32[2,8,128]{2,1,0:T(8,128)S(1)}) custom-call(f32[4,4,256,128]{3,2,1,0:T(8,128)} %get-tuple-element.61.late, bf16[3,352,256]{2,1,0:T(8,128)(2,1)} %get-tuple-element.62.feed_piece, ...), custom_call_target="tpu_custom_call" | custom-call | tf_op jit(solution)/shard_map/last/pallas_call | solution.py:1588
  258.0 6.4 %finish.1 = (bf16[512,1024]{1,0:T(8,128)(2,1)}, f32[512,1024]{1,0:T(8,128)}, f32[1024,256]{1,0:T(8,128)}, f32[1024,256]{1,0:T(8,128)}, f32[1024,256]{1,0:T(8,128...) custom-call(f32[512,1024]{1,0:T(8,128)S(1)} %get-tuple-element.77.gr, ...), custom_call_target="tpu_custom_call" | custom-call | tf_op jit(solution)/shard_map/finish/pallas_call | solution.py:1641
